TPU v7x, 768 devices: a whole 4x8x12 slice. The times are simulated.
768 devices in a mesh: ka: 192 (over x, z, y_lo), pt: 4 (over y_hi, core).
Axes of the slice: x: 4, y: 8 (y_hi: 2, y_lo: 4; y = y_hi * 4 + y_lo), z: 12, core: 2. Of those that a mesh axis runs over, the one named last changes fastest.
Arguments:
- orbitals: bfloat16 [192, 4096, 256], P('ka', 'pt'), may hold values from -6 to 6
- kernel: bfloat16 [192, 3, 256, 2, 4096], P('ka', None, None, None, 'pt'), may hold values from -0.00390625 to 0.00390625
- partners: int32 [192, 3], P('ka'), may hold values from 0 to 191, as said below
Outputs:
- exchanged: float32 [192, 256, 256], P('ka', 'pt')
Inputs may be any that keep to these rules, and one draw needn't show every extreme that they name: partners[k, t] = (k - s_t) mod 192 for 3 distinct shifts s_t of 1 to 7, the same for every k; one of the shifts is 7.
All inputs are finite; a program needn't handle non-finite values.
Results may differ from a plain program's by a relative error of at most 0.0029.
Values may be sent and summed in bfloat16 or wider, within the bound.
No kernel may reach another device: no remote copies, remote signals or barrier semaphores. Data moves between devices by JAX's collectives and lax.ppermute only.
A program may use at most 32 MiB of HBM per device.

v0:
```python
import jax
import jax.numpy as jnp
from jax import lax
from jax.sharding import PartitionSpec as P

MU_DEV = 64
TRANSFERS = 3
SPAN = 7


def passed_along(value, axis, steps):
    count = lax.axis_size(axis)
    pairs = [(source, (source + steps) % count) for source in range(count)]
    return lax.ppermute(value, axis, pairs)


def fetch_partners(payload, shifts):
    arrivals = jnp.stack([passed_along(payload, "ka", offset) for offset in range(1, SPAN + 1)])
    return [
        lax.dynamic_index_in_dim(arrivals, shifts[transfer] - 1, 0, keepdims=False)
        for transfer in range(TRANSFERS)
    ]


def shards(orbitals, kernel, partners):
    local_orbs = orbitals[0]
    points = local_orbs.shape[0]
    half_width = local_orbs.shape[1] // 2
    window = lax.all_gather(local_orbs[:MU_DEV], "pt", axis=0, tiled=True)
    payload = jnp.concatenate([local_orbs, window], 0)
    shifts = (lax.axis_index("ka") - partners[0]) % lax.axis_size("ka")
    fetched = fetch_partners(payload, shifts)
    turned = jnp.concatenate(
        [local_orbs, jnp.concatenate([-local_orbs[:, half_width:], local_orbs[:, :half_width]], 1)],
        0,
    )
    row_total = MU_DEV * lax.axis_size("pt")
    summed = jnp.zeros((row_total, 2 * half_width), jnp.float32)
    for transfer in range(TRANSFERS):
        arrived = fetched[transfer]
        partner_block = arrived[:points]
        window_part = lax.dynamic_slice_in_dim(arrived, points, row_total, 0)
        swapped = jnp.concatenate([window_part[:, half_width:], -window_part[:, :half_width]], 1)
        density = lax.dot_general(
            jnp.concatenate([window_part, swapped], 0),
            partner_block,
            (((1,), (1,)), ((), ())),
            preferred_element_type=jnp.float32,
        )
        density_real = density[:row_total]
        density_imag = density[row_total:]
        kernel_rows = kernel[0, transfer]
        kernel_real = kernel_rows[:, 0, :].astype(jnp.float32)
        kernel_imag = kernel_rows[:, 1, :].astype(jnp.float32)
        screened = jnp.concatenate(
            [
                kernel_real * density_real - kernel_imag * density_imag,
                kernel_real * density_imag + kernel_imag * density_real,
            ],
            1,
        ).astype(jnp.bfloat16)
        summed = summed + jnp.dot(screened, turned, preferred_element_type=jnp.float32)
    result = lax.psum_scatter(summed, "pt", scatter_dimension=0, tiled=True)
    return result[None]


def solution(mesh):
    in_specs = (P("ka", "pt", None), P("ka", None, None, None, "pt"), P("ka", None))
    out_specs = P("ka", "pt", None)
    return jax.shard_map(shards, mesh=mesh, in_specs=in_specs, out_specs=out_specs, check_vma=False)
```

profile of v0, /device:TPU:1, one launch (start us, length us, event | category | flops | bytes accessed | tf_op | source)
XLA Modules:
  0.0 321.7 jit_solution(10423131667396497715)
XLA Ops:
  6.5 0.0 reduce-scatter.2.cloned.1.call-start
  6.5 0.8 slice.107
  7.3 19.7 %all-gather = bf16[1,256,256]{2,1,0:T(8,128)(2,1)S(1)} all-gather(bf16[1,64,256]{2,1,0:T(8,128)(2,1)S(1)} %slice.107), channel_id=2, replica_groups=mesh['ka'=192,'pt'=4] {'pt'}, dimensions={1}, use_global_device_ids=true | all-gather | bytes 163840 | tf_op jit(solution)/shard_map/all_gather | solution.py:29
  27.0 2.0 pad_maximum_fusion
  28.9 1.9 collective-permute-start
  30.8 1.9 collective-permute-start.1
  32.8 1.9 collective-permute-start.2
  34.7 1.9 collective-permute-start.3
  36.6 3.6 %collective-permute-start.4 = (bf16[1280,256]{1,0:T(8,128)(2,1)}, bf16[1280,256]{1,0:T(8,128)(2,1)}, u32[]{:S(2)}, u32[]{:S(2)}) collective-permute-start(bf16[1280,256]{1,0:T(8,128)(2,1)} %pad_maximum_fusion), channel_id=1, source_target_pairs={{0,20},{4,24},{8,28},{12,32},{16,36},{20,40},{24,44},{28,48},{32,5... | collective-permute-start | bytes 1966088 | tf_op jit(solution)/shard_map/ppermute | solution.py:14
  40.3 0.0 copy-start.1
  40.3 4.3 %fusion.49 = (bf16[1,1,256,2,1024]{4,3,2,1,0:T(2,128)(2,1)S(1)}, bf16[1,1,256,2,1024]{4,3,2,1,0:T(2,128)(2,1)}, bf16[1,1,256,2,1024]{4,3,2,1,0:T(2,128)(2,1)S(1)}) fusion(bf16[1,3,256,2,1024]{4,3,2,1,0:T(2,128)(2,1)} %param.4), kind=kLoop, calls=%fused_computation.92 | loop fusion | bytes 6291456 | tf_op jit(solution)/shard_map/slice | solution.py:52
  44.6 0.0 copy-done.1
  44.6 0.7 fusion.53
  49.2 0.3 copy.13
  49.5 0.0 copy-start
  49.5 1.9 copy_bitcast_fusion
  51.4 0.0 copy-done
  51.5 0.1 slice_negate_fusion
  51.5 43.4 %collective-permute-done = bf16[1280,256]{1,0:T(8,128)(2,1)} collective-permute-done((bf16[1280,256]{1,0:T(8,128)(2,1)}, bf16[1280,256]{1,0:T(8,128)(2,1)}, u32[]{:S(2)}, u32[]{:S(2)}) %collective-permute-start) | collective-permute-done | bytes 655392 | tf_op jit(solution)/shard_map/ppermute | solution.py:14
  95.0 1.9 collective-permute-start.5
  96.9 1.1 bitcast_dynamic-update-slice_fusion.6
  98.0 0.0 collective-permute-done.1
  98.0 1.9 collective-permute-start.6
  99.9 1.1 bitcast_dynamic-update-slice_fusion.5
  101.1 0.0 collective-permute-done.2
  101.1 1.1 bitcast_dynamic-update-slice_fusion.4
  102.2 0.0 collective-permute-done.3
  102.2 1.1 bitcast_dynamic-update-slice_fusion.3
  103.4 44.2 %collective-permute-done.4 = bf16[1280,256]{1,0:T(8,128)(2,1)} collective-permute-done((bf16[1280,256]{1,0:T(8,128)(2,1)}, bf16[1280,256]{1,0:T(8,128)(2,1)}, u32[]{:S(2)}, u32[]{:S(2)}) %collective-permute-start.4) | collective-permute-done | bytes 655392 | tf_op jit(solution)/shard_map/ppermute | solution.py:14
  147.5 1.1 bitcast_dynamic-update-slice_fusion.2
  148.7 25.8 %collective-permute-done.5 = bf16[1280,256]{1,0:T(8,128)(2,1)S(1)} collective-permute-done((bf16[1280,256]{1,0:T(8,128)(2,1)}, bf16[1280,256]{1,0:T(8,128)(2,1)S(1)}, u32[]{:S(2)}, u32[]{:S(2)}) %collective-permute-start.5) | collective-permute-done | bytes 655392 | tf_op jit(solution)/shard_map/ppermute | solution.py:14
  174.5 0.1 collective-permute-done.6
  174.8 0.5 fusion.24
  175.2 0.5 fusion.1
  175.8 0.5 fusion.23
  176.2 0.4 fusion.5
  176.7 0.5 fusion.22
  177.1 0.4 fusion.9
  177.6 0.4 fusion.12
  178.0 0.4 convolution_add_fusion.1
  178.5 1.1 convolution_add_fusion
  179.6 0.0 reduce-scatter.2.cloned.1.call-update
  179.7 135.2 %reduce-scatter.2.cloned.1.call-done = f32[64,256]{1,0:T(8,128)} async-done(((f32[256,256]{1,0:T(8,128)}), f32[64,256]{1,0:T(8,128)}) %reduce-scatter.2.cloned.1.call-update) | async-done | bytes 65552 | tf_op jit(solution)/shard_map/reduce_scatter | solution.py:63
  (6 shorter events, 0.2 us)
Async XLA Ops:
  6.5 308.3 %reduce-scatter.2.cloned.1.call-start = ((), (), s32[]{:S(2)}) async-start(), calls=%async_computation.1 | async-start | bytes 327680 | tf_op jit(solution)/shard_map/reduce_scatter | solution.py:63
  28.9 66.0 %collective-permute-start = (bf16[1280,256]{1,0:T(8,128)(2,1)}, bf16[1280,256]{1,0:T(8,128)(2,1)}, u32[]{:S(2)}, u32[]{:S(2)}) collective-permute-start(bf16[1280,256]{1,0:T(8,128)(2,1)} %pad_maximum_fusion), channel_id=1, source_target_pairs={{0,4},{4,8},{8,12},{12,16},{16,20},{20,24},{24,28},{28,32},{32,36}... | collective-permute-start | bytes 1966088 | tf_op jit(solution)/shard_map/ppermute | solution.py:14
  30.8 67.2 %collective-permute-start.1 = (bf16[1280,256]{1,0:T(8,128)(2,1)}, bf16[1280,256]{1,0:T(8,128)(2,1)}, u32[]{:S(2)}, u32[]{:S(2)}) collective-permute-start(bf16[1280,256]{1,0:T(8,128)(2,1)} %pad_maximum_fusion), channel_id=1, source_target_pairs={{0,8},{4,12},{8,16},{12,20},{16,24},{20,28},{24,32},{28,36},{32,40... | collective-permute-start | bytes 1966088 | tf_op jit(solution)/shard_map/ppermute | solution.py:14
  32.8 68.3 %collective-permute-start.2 = (bf16[1280,256]{1,0:T(8,128)(2,1)}, bf16[1280,256]{1,0:T(8,128)(2,1)}, u32[]{:S(2)}, u32[]{:S(2)}) collective-permute-start(bf16[1280,256]{1,0:T(8,128)(2,1)} %pad_maximum_fusion), channel_id=1, source_target_pairs={{0,12},{4,16},{8,20},{12,24},{16,28},{20,32},{24,36},{28,40},{32,4... | collective-permute-start | bytes 1966088 | tf_op jit(solution)/shard_map/ppermute | solution.py:14
  34.7 67.5 %collective-permute-start.3 = (bf16[1280,256]{1,0:T(8,128)(2,1)}, bf16[1280,256]{1,0:T(8,128)(2,1)}, u32[]{:S(2)}, u32[]{:S(2)}) collective-permute-start(bf16[1280,256]{1,0:T(8,128)(2,1)} %pad_maximum_fusion), channel_id=1, source_target_pairs={{0,16},{4,20},{8,24},{12,28},{16,32},{20,36},{24,40},{28,44},{32,4... | collective-permute-start | bytes 1966088 | tf_op jit(solution)/shard_map/ppermute | solution.py:14
  36.6 110.9 %collective-permute-start.4 = (bf16[1280,256]{1,0:T(8,128)(2,1)}, bf16[1280,256]{1,0:T(8,128)(2,1)}, u32[]{:S(2)}, u32[]{:S(2)}) collective-permute-start(bf16[1280,256]{1,0:T(8,128)(2,1)} %pad_maximum_fusion), channel_id=1, source_target_pairs={{0,20},{4,24},{8,28},{12,32},{16,36},{20,40},{24,44},{28,48},{32,5... | collective-permute-start | bytes 1966088 | tf_op jit(solution)/shard_map/ppermute | solution.py:14
  40.3 4.4 %copy-start.1 = (s32[1,3]{1,0:T(1,128)S(1)}, s32[1,3]{1,0:T(1,128)}, u32[]{:S(2)}) copy-start(s32[1,3]{1,0:T(1,128)} %param.5) | copy-start | bytes 40
  49.5 1.9 copy-start
  95.0 79.5 %collective-permute-start.5 = (bf16[1280,256]{1,0:T(8,128)(2,1)}, bf16[1280,256]{1,0:T(8,128)(2,1)S(1)}, u32[]{:S(2)}, u32[]{:S(2)}) collective-permute-start(bf16[1280,256]{1,0:T(8,128)(2,1)} %pad_maximum_fusion), channel_id=1, source_target_pairs={{0,24},{4,28},{8,32},{12,36},{16,40},{20,44},{24,48},{28,52},{32,5... | collective-permute-start | bytes 1966088 | tf_op jit(solution)/shard_map/ppermute | solution.py:14
  98.0 76.6 %collective-permute-start.6 = (bf16[1280,256]{1,0:T(8,128)(2,1)}, bf16[1280,256]{1,0:T(8,128)(2,1)S(1)}, u32[]{:S(2)}, u32[]{:S(2)}) collective-permute-start(bf16[1280,256]{1,0:T(8,128)(2,1)} %pad_maximum_fusion), channel_id=1, source_target_pairs={{0,28},{4,32},{8,36},{12,40},{16,44},{20,48},{24,52},{28,56},{32,6... | collective-permute-start | bytes 1966088 | tf_op jit(solution)/shard_map/ppermute | solution.py:14
Sparse Core Ops, SparseCore 0:
  179.8 134.9 reduce-scatter.1
where the time goes:
time: 322 us
  waiting for transfers between devices  249 us (77%)
  blocking collectives  19.7 us (6%)
  between operations  17.5 us (5%)
  starting transfers between devices  15.1 us (5%)
  local copies, waits for them, and re-layouts  13.8 us (4%)
  matrix products  3.46 us (1%)
  other arithmetic  3.41 us (1%)
    reduce_scatter x1, waiting for transfers between devices, shards(): result = lax.psum_scatter(summed, 'pt', scatter_dimension=0, tiled=True)  135 us
    ppermute x7, waiting for transfers between devices, passed_along(): return lax.ppermute(value, axis, pairs)  114 us
    all_gather x1, blocking collectives, shards(): window = lax.all_gather(local_orbs[:MU_DEV], 'pt', axis=0, tiled=True)  19.7 us
    ppermute x7, starting transfers between devices, passed_along(): return lax.ppermute(value, axis, pairs)  15.1 us
  transfers between devices with their start and end apart: 8, of which 5 were waited for; matrix products, arithmetic and copies ran while one was open for 4% of the time, Pallas kernels for 0%

commit v1 on v0

v1 whole, which is shorter than its diff:
```python
import functools

import jax
import jax.numpy as jnp
from jax import lax
from jax.experimental import pallas as pl
from jax.experimental.pallas import tpu as pltpu
from jax.sharding import PartitionSpec as P

MU_DEV = 64
TRANSFERS = 3
SPAN = 7
COLUMNS = 512

ROUTES = {
    (1, 2): {1: (0, 1), 2: (1, 1)},
    (2, 3): {3: (0, 3), 2: (3, -1)},
    (1, 5): {1: (0, 1), 5: (1, 4)},
    (2, 5): {1: (0, 1), 2: (1, 1), 5: (1, 4)},
    (4, 5): {4: (0, 4), 5: (4, 1)},
    (2, 6): {2: (0, 2), 6: (2, 4)},
    (3, 6): {3: (0, 3), 6: (3, 3)},
    (4, 6): {4: (0, 4), 6: (4, 2)},
    (5, 6): {5: (0, 5), 6: (5, 1)},
}


def passed_along(value, axis, steps):
    count = lax.axis_size(axis)
    pairs = [(source, (source + steps) % count) for source in range(count)]
    return lax.ppermute(value, axis, pairs)


def summed_over(partial, axis):
    count = lax.axis_size(axis)
    blocks = partial.reshape(count, partial.shape[0] // count, partial.shape[1])
    return jnp.sum(lax.all_to_all(blocks, axis, 0, 0), 0)


def arrivals(low, high, local_orbs):
    others = others_of(local_orbs[:MU_DEV], "pt")
    routes = ROUTES.get((low, high), {low: (0, low), high: (0, high)})
    held = {0: jnp.concatenate([local_orbs, others], 0)}
    for shift, (source, steps) in routes.items():
        held[shift] = passed_along(held[source], "ka", steps)
    return held[low], held[high], passed_along(others, "ka", SPAN)


def others_of(rows, axis):
    window = lax.all_gather(rows, axis, axis=0, tiled=True)
    start = (lax.axis_index(axis) + 1) * rows.shape[0]
    size = window.shape[0] - rows.shape[0]
    return lax.dynamic_slice_in_dim(jnp.concatenate([window, window], 0), start, size, 0)


def exchange_kernel(places_ref, far_ref, rest_ref, low_ref, high_ref, plane_ref, orbs_ref, out_ref, window_ref):
    transfer = pl.program_id(0)
    tile = pl.program_id(1)
    width = orbs_ref.shape[1]
    half_width = width // 2
    row_total = out_ref.shape[0]
    count = row_total // MU_DEV
    points = far_ref.shape[0]
    here = places_ref[TRANSFERS]
    columns = pl.ds(pl.multiple_of(tile * COLUMNS, COLUMNS), COLUMNS)

    def take_window(block_ref, others_ref, first_row):
        for steps in range(count):
            at = pl.multiple_of(lax.rem(here + steps, count) * MU_DEV, MU_DEV)
            start = first_row + (steps - 1) * MU_DEV
            rows = others_ref[start:start + MU_DEV, :] if steps else block_ref[0:MU_DEV, :]
            window_ref[pl.ds(at, MU_DEV), :] = rows
            window_ref[pl.ds(row_total + at, MU_DEV), 0:half_width] = rows[:, half_width:]
            window_ref[pl.ds(row_total + at, MU_DEV), half_width:width] = -rows[:, :half_width]

    def add_columns(block_ref):
        density = lax.dot_general(
            window_ref[...], block_ref[columns, :], (((1,), (1,)), ((), ())),
            preferred_element_type=jnp.float32,
        )
        density_real = density[:row_total]
        density_imag = density[row_total:]
        kernel_real = plane_ref[0, 0].astype(jnp.float32)
        kernel_imag = plane_ref[0, 1].astype(jnp.float32)
        screened_real = (kernel_real * density_real - kernel_imag * density_imag).astype(jnp.bfloat16)
        screened_imag = (kernel_real * density_imag + kernel_imag * density_real).astype(jnp.bfloat16)
        orbs = orbs_ref[columns, :]
        turned = jnp.concatenate([-orbs[:, half_width:], orbs[:, :half_width]], 1)
        out_ref[...] += jnp.dot(screened_real, orbs, preferred_element_type=jnp.float32) + jnp.dot(
            screened_imag, turned, preferred_element_type=jnp.float32
        )

    @pl.when((transfer == 0) & (tile == 0))
    def _():
        out_ref[...] = jnp.zeros_like(out_ref)

    arrived = ((far_ref, rest_ref, 0), (low_ref, low_ref, points), (high_ref, high_ref, points))
    for at, (block_ref, others_ref, first_row) in enumerate(arrived):

        @pl.when((transfer == at) & (tile == 0))
        def _(block_ref=block_ref, others_ref=others_ref, first_row=first_row):
            take_window(block_ref, others_ref, first_row)

        @pl.when(transfer == at)
        def _(block_ref=block_ref):
            add_columns(block_ref)


def exchanged_here(places, farthest, rest, low, high, planes, orbs):
    row_total, points = planes.shape[2:]
    width = orbs.shape[1]
    whole = pl.BlockSpec(memory_space=pltpu.VMEM)
    return pl.pallas_call(
        exchange_kernel,
        out_shape=jax.ShapeDtypeStruct((row_total, width), jnp.float32),
        grid_spec=pltpu.PrefetchScalarGridSpec(
            num_scalar_prefetch=1,
            grid=(TRANSFERS, points // COLUMNS),
            in_specs=[
                whole,
                whole,
                whole,
                whole,
                pl.BlockSpec((1, 2, row_total, COLUMNS), lambda t, c, places: (places[t], 0, 0, c)),
                whole,
            ],
            out_specs=pl.BlockSpec((row_total, width), lambda t, c, places: (0, 0)),
            scratch_shapes=[pltpu.VMEM((2 * row_total, width), jnp.bfloat16)],
        ),
        compiler_params=pltpu.CompilerParams(vmem_limit_bytes=24 * 2**20),
        cost_estimate=pl.CostEstimate(
            flops=2 * TRANSFERS * 4 * row_total * points * width,
            bytes_accessed=2 * planes.size + 2 * TRANSFERS * low.size,
            transcendentals=0,
        ),
    )(places, farthest, rest, low, high, planes, orbs)


def shards(orbitals, kernel, partners):
    local_orbs = orbitals[0]
    farthest = passed_along(local_orbs, "ka", SPAN)
    payload, planes = lax.optimization_barrier((local_orbs, kernel[0].transpose(0, 2, 1, 3)))
    here = lax.axis_index("ka")
    count = lax.axis_size("ka")
    shifts = [(here - partners[0, t] + count) % count for t in range(TRANSFERS)]
    smaller = [jnp.where(s == SPAN, 0, s) for s in shifts]
    high = jnp.maximum(jnp.maximum(smaller[0], smaller[1]), smaller[2])
    low = smaller[0] + smaller[1] + smaller[2] - high
    places = [
        jnp.where(shifts[1] == s, 1, 0) + jnp.where(shifts[2] == s, 2, 0) for s in (SPAN, low, high)
    ]
    places = jnp.stack(places + [lax.axis_index("pt")]).astype(jnp.int32)
    pairs = [(first, second) for second in range(2, SPAN) for first in range(1, second)]
    which = lax.shift_right_logical((high - 1) * (high - 2), 1) + low - 1
    branches = [functools.partial(arrivals, first, second) for first, second in pairs]
    from_low, from_high, rest = lax.switch(which, branches, payload)
    summed = exchanged_here(places, farthest, rest, from_low, from_high, planes, local_orbs)
    return summed_over(summed, "pt")[None]


def solution(mesh):
    in_specs = (P("ka", "pt", None), P("ka", None, None, None, "pt"), P("ka", None))
    out_specs = P("ka", "pt", None)
    return jax.shard_map(shards, mesh=mesh, in_specs=in_specs, out_specs=out_specs, check_vma=False)
```

time: 322 us -> 107 us (0.33)
  waiting for transfers between devices: 249 us -> 41.6 us
  between operations: 17.5 us -> 1.98 us
  blocking collectives: 19.7 us -> 35.1 us
  local copies, waits for them, and re-layouts: 13.8 us -> 5.04 us
  Pallas kernels: 0 us -> 7.41 us
  matrix products: 3.46 us -> 0 us
    reduce_scatter x1 -> x0, waiting for transfers between devices: 135 us -> none  [shards(): result = lax.psum_scatter(summed, 'pt', scatter_dimension=0, tiled=True)]
    ppermute x7 -> x4, waiting for transfers between devices: 114 us -> 41.6 us  [passed_along(): return lax.ppermute(value, axis, pairs)]
    all_to_all x0 -> x1, blocking collectives: none -> 14.4 us  [summed_over(): return jnp.sum(lax.all_to_all(blocks, axis, 0, 0), 0)]
    pallas_call x0 -> x1, Pallas kernels: none -> 7.41 us  [exchanged_here(): pl.pallas_call(exchange_kernel, out_shape=jax.ShapeDtypeStruct((row_total...]
    slice x3 -> x2, local copies, waits for them, and re-layouts: 5.77 us -> 2.18 us  [the longest x1 1.42 us: shards(): shifts = [(here - partners[0, t] + count) % count for t in range(TRANSFERS)]]
    dot_general x6 -> x0, matrix products: 3.46 us -> none  [the longest x3 2.04 us: shards(): jnp.dot(screened, turned, preferred_element_type=jnp.float32)]
    ppermute x7 -> x4, starting transfers between devices: 15.1 us -> 13.6 us  [passed_along(): return lax.ppermute(value, axis, pairs)]
  transfers between devices with their start and end apart: 8 -> 4, of which waited for: 5 -> 2; matrix products, arithmetic and copies ran while one was open for 4% -> 6% of each run, Pallas kernels for 0% -> 0%
where the time goes in v1:
time: 107 us
  waiting for transfers between devices  41.6 us (39%)
  blocking collectives  35.1 us (33%)
  starting transfers between devices  13.6 us (13%)
  Pallas kernels  7.41 us (7%)
  local copies, waits for them, and re-layouts  5.04 us (5%)
  other arithmetic  2 us (2%)
  between operations  1.98 us (2%)
    ppermute x4, waiting for transfers between devices, passed_along(): return lax.ppermute(value, axis, pairs)  41.6 us
    all_gather x1, blocking collectives, others_of(): window = lax.all_gather(rows, axis, axis=0, tiled=True)  20.7 us
    all_to_all x1, blocking collectives, summed_over(): return jnp.sum(lax.all_to_all(blocks, axis, 0, 0), 0)  14.4 us
    ppermute x4, starting transfers between devices, passed_along(): return lax.ppermute(value, axis, pairs)  13.6 us
    pallas_call x1, Pallas kernels, exchanged_here(): pl.pallas_call(exchange_kernel, out_shape=jax.ShapeDtypeStruct((row_total...  7.41 us
    unnamed x1, local copies, waits for them, and re-layouts  2.86 us
  transfers between devices with their start and end apart: 4, of which 2 were waited for; matrix products, arithmetic and copies ran while one was open for 6% of the time, Pallas kernels for 0%

profile of v1, /device:TPU:1, one launch (start us, length us, event | category | flops | bytes accessed | tf_op | source)
XLA Modules:
  0.0 106.8 jit_solution(342078974357757816)
XLA Ops:
  0.0 7.9 %collective-permute-start.46 = (bf16[1024,256]{1,0:T(8,128)(2,1)}, bf16[1024,256]{1,0:T(8,128)(2,1)}, u32[]{:S(2)}, u32[]{:S(2)}) collective-permute-start(bf16[1024,256]{1,0:T(8,128)(2,1)} %bitcast.17), channel_id=1, source_target_pairs={{0,28},{4,32},{8,36},{12,40},{16,44},{20,48},{24,52},{28,56},{32,6... | collective-permute-start | bytes 1572872 | tf_op jit(solution)/shard_map/ppermute | solution.py:31
  7.9 1.4 %fusion.15 = (s32[1,1]{1,0:T(1,128)}, s32[1,1]{1,0:T(1,128)}, s32[1,1]{1,0:T(1,128)}) fusion(s32[1,3]{1,0:T(1,128)} %param.20), kind=kLoop, calls=%fused_computation.62 | loop fusion | bytes 24 | tf_op jit(solution)/shard_map/slice | solution.py:145
  11.2 2.9 %copy.6 = bf16[1,3,256,2,1024]{4,2,3,1,0:T(8,128)(2,1)S(1)} copy(bf16[1,3,256,2,1024]{4,3,2,1,0:T(2,128)(2,1)} %param.19) | data formatting | bytes 6291456 | tf_op args[1]
  14.1 70.1 %conditional.1 = (bf16[1216,256]{1,0:T(8,128)(2,1)}, bf16[1216,256]{1,0:T(8,128)(2,1)}, bf16[192,256]{1,0:T(8,128)(2,1)}) conditional(s32[]{:T(128)} %clamp.3, bf16[1024,256]{1,0:T(8,128)(2,1)} %bitcast.18, bf16[1024,256]{1,0:T(8,128)(2,1)} %bitcast.19, bf16[1024,256]{1,0:T(8,128)(2,1)} %bitcast.20, ...), branch_computations={%region_0.1_spmd, %region_1.2_spmd, %region_2.3_spmd, %region_3.4_... | conditional | flops 1441799 | bytes 9568522 | solution.py:156
  14.1 0.8 slice.39
  14.9 20.7 %all_gather.33 = bf16[256,256]{1,0:T(8,128)(2,1)S(1)} all-gather(bf16[64,256]{1,0:T(8,128)(2,1)S(1)} %slice.39), channel_id=1, replica_groups=mesh['ka'=192,'pt'=4] {'pt'}, dimensions={0}, use_global_device_ids=true | all-gather | bytes 163840 | tf_op jit(solution)/shard_map/cond/branch_3_fun/all_gather | solution.py:50
  35.6 0.2 fusion.3
  35.8 1.1 %pad_maximum_fusion.3 = bf16[1216,256]{1,0:T(8,128)(2,1)S(1)} fusion(bf16[192,256]{1,0:T(8,128)(2,1)S(1)} %fusion.3, bf16[1024,256]{1,0:T(8,128)(2,1)} %param.3), kind=kLoop, calls=%fused_computation.12 | loop fusion | flops 1245184 | bytes 1245184 | tf_op jit(solution)/shard_map/cond/branch_3_fun/concatenate | solution.py:43
  36.9 1.9 %collective-permute-start.10 = (bf16[1216,256]{1,0:T(8,128)(2,1)S(1)}, bf16[1216,256]{1,0:T(8,128)(2,1)}, u32[]{:S(2)}, u32[]{:S(2)}) collective-permute-start(bf16[1216,256]{1,0:T(8,128)(2,1)S(1)} %pad_maximum_fusion.3), channel_id=1, source_target_pairs={{0,16},{4,20},{8,24},{12,28},{16,32},{20,36},{24,40},{28,44},{32,4... | collective-permute-start | bytes 1867784 | tf_op jit(solution)/shard_map/cond/branch_3_fun/ppermute | solution.py:31
  38.8 1.9 %collective-permute-start.9 = (bf16[1216,256]{1,0:T(8,128)(2,1)S(1)}, bf16[1216,256]{1,0:T(8,128)(2,1)}, u32[]{:S(2)}, u32[]{:S(2)}) collective-permute-start(bf16[1216,256]{1,0:T(8,128)(2,1)S(1)} %pad_maximum_fusion.3), channel_id=1, source_target_pairs={{0,4},{4,8},{8,12},{12,16},{16,20},{20,24},{24,28},{28,32},{32,36}... | collective-permute-start | bytes 1867784 | tf_op jit(solution)/shard_map/cond/branch_3_fun/ppermute | solution.py:31
  40.7 1.9 %collective-permute-start.11 = (bf16[192,256]{1,0:T(8,128)(2,1)S(1)}, bf16[192,256]{1,0:T(8,128)(2,1)}, u32[]{:S(2)}, u32[]{:S(2)}) collective-permute-start(bf16[192,256]{1,0:T(8,128)(2,1)S(1)} %fusion.3), channel_id=1, source_target_pairs={{0,28},{4,32},{8,36},{12,40},{16,44},{20,48},{24,52},{28,56},{32,6... | collective-permute-start | bytes 294920 | tf_op jit(solution)/shard_map/cond/branch_3_fun/ppermute | solution.py:31
  42.7 18.2 %collective-permute-done.11 = bf16[192,256]{1,0:T(8,128)(2,1)} collective-permute-done((bf16[192,256]{1,0:T(8,128)(2,1)S(1)}, bf16[192,256]{1,0:T(8,128)(2,1)}, u32[]{:S(2)}, u32[]{:S(2)}) %collective-permute-start.11) | collective-permute-done | bytes 98336 | tf_op jit(solution)/shard_map/cond/branch_3_fun/ppermute | solution.py:31
  60.8 0.0 collective-permute-done.10
  60.8 23.4 %collective-permute-done.9 = bf16[1216,256]{1,0:T(8,128)(2,1)} collective-permute-done((bf16[1216,256]{1,0:T(8,128)(2,1)S(1)}, bf16[1216,256]{1,0:T(8,128)(2,1)}, u32[]{:S(2)}, u32[]{:S(2)}) %collective-permute-start.9) | collective-permute-done | bytes 622624 | tf_op jit(solution)/shard_map/cond/branch_3_fun/ppermute | solution.py:31
  84.2 0.1 pad_add_fusion.places_ref
  84.3 0.0 collective-permute-done.46.far_ref
  84.3 7.4 %shard_map.37 = f32[256,256]{1,0:T(8,128)S(1)} custom-call(s32[4]{0:T(128)S(1)} %pad_add_fusion.places_ref, bf16[1024,256]{1,0:T(8,128)(2,1)} %collective-permute-done.46.far_ref, bf16[192,256]{1,0:T(8,128)(2,1)} %get-tuple-element.26.rest_ref, bf16[1216,256]{1,0:T(8,128)(2,1)} %get-tuple-element.27.low_ref, bf16[1216,256]{1,0:T(8,128)(2,1)} %get-tuple-element.28.high_ref, ...), custom_call_target="tpu_custom_call" | custom-call | flops 1610612736 | bytes 5013504 | tf_op jit(solution)/shard_map/pallas_call | solution.py:113
  91.7 14.4 %all_to_all.5 = f32[4,64,256]{2,1,0:T(8,128)S(1)} all-to-all(f32[4,64,256]{2,1,0:T(8,128)S(1)} %bitcast.16), channel_id=1, replica_groups=mesh['ka'=192,'pt'=4] {'pt'}, dimensions={0} | all-to-all | bytes 524288 | tf_op jit(solution)/shard_map/all_to_all | solution.py:37
  106.1 0.6 reduce_sum.9
Async XLA Ops:
  0.0 84.3 %collective-permute-start.46 = (bf16[1024,256]{1,0:T(8,128)(2,1)}, bf16[1024,256]{1,0:T(8,128)(2,1)}, u32[]{:S(2)}, u32[]{:S(2)}) collective-permute-start(bf16[1024,256]{1,0:T(8,128)(2,1)} %bitcast.17), channel_id=1, source_target_pairs={{0,28},{4,32},{8,36},{12,40},{16,44},{20,48},{24,52},{28,56},{32,6... | collective-permute-start | bytes 1572872 | tf_op jit(solution)/shard_map/ppermute | solution.py:31
  36.9 24.0 %collective-permute-start.10 = (bf16[1216,256]{1,0:T(8,128)(2,1)S(1)}, bf16[1216,256]{1,0:T(8,128)(2,1)}, u32[]{:S(2)}, u32[]{:S(2)}) collective-permute-start(bf16[1216,256]{1,0:T(8,128)(2,1)S(1)} %pad_maximum_fusion.3), channel_id=1, source_target_pairs={{0,16},{4,20},{8,24},{12,28},{16,32},{20,36},{24,40},{28,44},{32,4... | collective-permute-start | bytes 1867784 | tf_op jit(solution)/shard_map/cond/branch_3_fun/ppermute | solution.py:31
  38.8 45.4 %collective-permute-start.9 = (bf16[1216,256]{1,0:T(8,128)(2,1)S(1)}, bf16[1216,256]{1,0:T(8,128)(2,1)}, u32[]{:S(2)}, u32[]{:S(2)}) collective-permute-start(bf16[1216,256]{1,0:T(8,128)(2,1)S(1)} %pad_maximum_fusion.3), channel_id=1, source_target_pairs={{0,4},{4,8},{8,12},{12,16},{16,20},{20,24},{24,28},{28,32},{32,36}... | collective-permute-start | bytes 1867784 | tf_op jit(solution)/shard_map/cond/branch_3_fun/ppermute | solution.py:31
  40.7 20.1 %collective-permute-start.11 = (bf16[192,256]{1,0:T(8,128)(2,1)S(1)}, bf16[192,256]{1,0:T(8,128)(2,1)}, u32[]{:S(2)}, u32[]{:S(2)}) collective-permute-start(bf16[192,256]{1,0:T(8,128)(2,1)S(1)} %fusion.3), channel_id=1, source_target_pairs={{0,28},{4,32},{8,36},{12,40},{16,44},{20,48},{24,52},{28,56},{32,6... | collective-permute-start | bytes 294920 | tf_op jit(solution)/shard_map/cond/branch_3_fun/ppermute | solution.py:31

commit v2 on v0

v2 whole, which is shorter than its diff:
```python
import functools

import jax
import jax.numpy as jnp
from jax import lax
from jax.experimental import pallas as pl
from jax.experimental.pallas import tpu as pltpu
from jax.sharding import PartitionSpec as P

MU_DEV = 64
TRANSFERS = 3
SPAN = 7
COLUMNS = 256

FIRST = 3
ROUTES = {
    (1, 2): ((2, 3), (1, 2)),
    (1, 3): ((1, 0),),
    (2, 3): ((2, 3),),
    (1, 4): ((2, 3), (4, 0), (1, 2)),
    (2, 4): ((2, 3), (4, 0)),
    (3, 4): ((4, 0),),
    (1, 5): ((1, 0), (5, 1)),
    (2, 5): ((2, 3), (5, 2)),
    (3, 5): ((2, 3), (5, 2)),
    (4, 5): ((4, 0), (5, 4)),
    (1, 6): ((6, 3), (1, 0)),
    (2, 6): ((6, 3), (2, 3)),
    (3, 6): ((6, 3),),
    (4, 6): ((6, 3), (4, 0)),
    (5, 6): ((6, 3), (5, 6)),
}


def passed_along(value, axis, steps):
    count = lax.axis_size(axis)
    pairs = [(source, (source + steps) % count) for source in range(count)]
    return lax.ppermute(value, axis, pairs)


def summed_over(partial, axis):
    count = lax.axis_size(axis)
    blocks = partial.reshape(count, partial.shape[0] // count, partial.shape[1])
    return jnp.sum(lax.all_to_all(blocks, axis, 0, 0).astype(jnp.float32), 0)


def arrivals(low, high, own, first):
    held = {0: own, FIRST: first}
    for shift, source in ROUTES[low, high]:
        held[shift] = passed_along(held[source], "ka", shift - source)
    return held[low], held[high]


def windows_of(blocks, axis):
    rows = jnp.concatenate([block[:MU_DEV] for block in blocks], 1)
    return lax.all_gather(rows, axis, axis=0, tiled=True)


def exchange_kernel(
    places_ref, far_ref, low_ref, high_ref, rows_ref, plane_ref, orbs_ref, out_ref, window_ref, sum_ref
):
    transfer = pl.program_id(0)
    points, width = orbs_ref.shape
    half_width = width // 2
    row_total = sum_ref.shape[0]

    def add_transfer(at, block_ref):
        real = rows_ref[:, at * width:at * width + half_width]
        imag = rows_ref[:, at * width + half_width:(at + 1) * width]
        window_ref[0:row_total, 0:half_width] = real
        window_ref[0:row_total, half_width:width] = imag
        window_ref[row_total:2 * row_total, 0:half_width] = imag
        window_ref[row_total:2 * row_total, half_width:width] = -real
        total = sum_ref[...]
        for tile in range(points // COLUMNS):
            columns = slice(tile * COLUMNS, (tile + 1) * COLUMNS)
            density = lax.dot_general(
                window_ref[...], block_ref[columns, :], (((1,), (1,)), ((), ())),
                preferred_element_type=jnp.float32,
            )
            density_real = density[:row_total]
            density_imag = density[row_total:]
            kernel_real = plane_ref[0, 0, :, columns].astype(jnp.float32)
            kernel_imag = plane_ref[0, 1, :, columns].astype(jnp.float32)
            screened_real = (kernel_real * density_real - kernel_imag * density_imag).astype(jnp.bfloat16)
            screened_imag = (kernel_real * density_imag + kernel_imag * density_real).astype(jnp.bfloat16)
            orbs = orbs_ref[columns, :]
            turned = jnp.concatenate([-orbs[:, half_width:], orbs[:, :half_width]], 1)
            total = total + jnp.dot(screened_real, orbs, preferred_element_type=jnp.float32)
            total = total + jnp.dot(screened_imag, turned, preferred_element_type=jnp.float32)
        sum_ref[...] = total

    @pl.when(transfer == 0)
    def _():
        sum_ref[...] = jnp.zeros_like(sum_ref)

    for at, block_ref in enumerate((far_ref, low_ref, high_ref)):

        @pl.when(transfer == at)
        def _(at=at, block_ref=block_ref):
            add_transfer(at, block_ref)

    @pl.when(transfer == TRANSFERS - 1)
    def _():
        out_ref[...] = sum_ref[...].astype(out_ref.dtype)


def exchanged_here(places, blocks, windows, planes, orbs):
    row_total, points = planes.shape[2:]
    width = orbs.shape[1]
    whole = pl.BlockSpec(memory_space=pltpu.VMEM)
    return pl.pallas_call(
        exchange_kernel,
        out_shape=jax.ShapeDtypeStruct((row_total, width), jnp.bfloat16),
        grid_spec=pltpu.PrefetchScalarGridSpec(
            num_scalar_prefetch=1,
            grid=(TRANSFERS,),
            in_specs=[whole] * (TRANSFERS + 1)
            + [pl.BlockSpec((1, 2, row_total, points), lambda t, places: (places[t], 0, 0, 0)), whole],
            out_specs=pl.BlockSpec((row_total, width), lambda t, places: (0, 0)),
            scratch_shapes=[
                pltpu.VMEM((2 * row_total, width), jnp.bfloat16),
                pltpu.VMEM((row_total, width), jnp.float32),
            ],
        ),
        compiler_params=pltpu.CompilerParams(vmem_limit_bytes=32 * 2**20),
        cost_estimate=pl.CostEstimate(
            flops=2 * TRANSFERS * 4 * row_total * points * width,
            bytes_accessed=2 * planes.size + 2 * TRANSFERS * orbs.size,
            transcendentals=0,
        ),
    )(places, *blocks, windows, planes, orbs)


def shards(orbitals, kernel, partners):
    local_orbs = orbitals[0]
    here = lax.axis_index("ka")
    count = lax.axis_size("ka")
    shifts = [(here - partners[0, t] + count) % count for t in range(TRANSFERS)]
    smaller = [jnp.where(s == SPAN, 0, s) for s in shifts]
    high = jnp.maximum(jnp.maximum(smaller[0], smaller[1]), smaller[2])
    low = smaller[0] + smaller[1] + smaller[2] - high
    places = [
        jnp.where(shifts[1] == s, 1, 0) + jnp.where(shifts[2] == s, 2, 0) for s in (SPAN, low, high)
    ]
    places = jnp.stack(places).astype(jnp.int32)
    which = lax.shift_right_logical((high - 1) * (high - 2), 1) + low - 1

    first = passed_along(local_orbs, "ka", FIRST)
    first, planes, places, which = lax.optimization_barrier(
        (first, kernel[0].transpose(0, 2, 1, 3), places, which)
    )
    farthest = passed_along(first, "ka", SPAN - FIRST)
    pairs = [(less, more) for more in range(2, SPAN) for less in range(1, more)]
    branches = [functools.partial(arrivals, less, more) for less, more in pairs]
    from_low, from_high = lax.switch(which, branches, local_orbs, first)
    blocks = (farthest, from_low, from_high)
    summed = exchanged_here(places, blocks, windows_of(blocks, "pt"), planes, local_orbs)
    return summed_over(summed, "pt")[None]


def solution(mesh):
    in_specs = (P("ka", "pt", None), P("ka", None, None, None, "pt"), P("ka", None))
    out_specs = P("ka", "pt", None)
    return jax.shard_map(shards, mesh=mesh, in_specs=in_specs, out_specs=out_specs, check_vma=False)
```

time: 322 us -> 101 us (0.31)
  waiting for transfers between devices: 249 us -> 36.1 us
  between operations: 17.5 us -> 2.01 us
  starting transfers between devices: 15.1 us -> 24.9 us
  local copies, waits for them, and re-layouts: 13.8 us -> 6.57 us
  blocking collectives: 19.7 us -> 25.2 us
  Pallas kernels: 0 us -> 5.1 us
  matrix products: 3.46 us -> 0 us
    reduce_scatter x1 -> x0, waiting for transfers between devices: 135 us -> none  [shards(): result = lax.psum_scatter(summed, 'pt', scatter_dimension=0, tiled=True)]
    ppermute x7 -> x4, waiting for transfers between devices: 114 us -> 36.1 us  [passed_along(): return lax.ppermute(value, axis, pairs)]
    all_to_all x0 -> x1, blocking collectives: none -> 11.9 us  [summed_over(): return jnp.sum(lax.all_to_all(blocks, axis, 0, 0).astype(jnp.float32), 0)]
    ppermute x7 -> x4, starting transfers between devices: 15.1 us -> 24.9 us  [passed_along(): return lax.ppermute(value, axis, pairs)]
    all_gather x1, blocking collectives: 19.7 us -> 13.3 us  [windows_of(): return lax.all_gather(rows, axis, axis=0, tiled=True)]
    pallas_call x0 -> x1, Pallas kernels: none -> 5.1 us  [exchanged_here(): pl.pallas_call(exchange_kernel, out_shape=jax.ShapeDtypeStruct((row_total...]
    dot_general x6 -> x0, matrix products: 3.46 us -> none  [the longest x3 2.04 us: shards(): jnp.dot(screened, turned, preferred_element_type=jnp.float32)]
  transfers between devices with their start and end apart: 8 -> 4, of which waited for: 5 -> 3; matrix products, arithmetic and copies ran while one was open for 4% -> 6% of each run, Pallas kernels for 0% -> 0%
where the time goes in v2:
time: 101 us
  waiting for transfers between devices  36.1 us (36%)
  blocking collectives  25.2 us (25%)
  starting transfers between devices  24.9 us (25%)
  local copies, waits for them, and re-layouts  6.57 us (7%)
  Pallas kernels  5.1 us (5%)
  between operations  2.01 us (2%)
    ppermute x4, waiting for transfers between devices, passed_along(): return lax.ppermute(value, axis, pairs)  36.1 us
    ppermute x4, starting transfers between devices, passed_along(): return lax.ppermute(value, axis, pairs)  24.9 us
    all_gather x1, blocking collectives, windows_of(): return lax.all_gather(rows, axis, axis=0, tiled=True)  13.3 us
    all_to_all x1, blocking collectives, summed_over(): return jnp.sum(lax.all_to_all(blocks, axis, 0, 0).astype(jnp.float32), 0)  11.9 us
    pallas_call x1, Pallas kernels, exchanged_here(): pl.pallas_call(exchange_kernel, out_shape=jax.ShapeDtypeStruct((row_total...  5.1 us
    unnamed x1, local copies, waits for them, and re-layouts  2.86 us
    slice x3, local copies, waits for them, and re-layouts, windows_of(): rows = jnp.concatenate([block[:MU_DEV] for block in blocks], 1)  2.29 us
  transfers between devices with their start and end apart: 4, of which 3 were waited for; matrix products, arithmetic and copies ran while one was open for 6% of the time, Pallas kernels for 0%

profile of v2, /device:TPU:1, one launch (start us, length us, event | category | flops | bytes accessed | tf_op | source)
XLA Modules:
  0.0 100.7 jit_solution(5656115665520810751)
XLA Ops:
  0.0 6.1 %collective-permute-start.27 = (bf16[1024,256]{1,0:T(8,128)(2,1)}, bf16[1024,256]{1,0:T(8,128)(2,1)}, u32[]{:S(2)}, u32[]{:S(2)}) collective-permute-start(bf16[1024,256]{1,0:T(8,128)(2,1)} %bitcast.16), channel_id=1, source_target_pairs={{0,12},{4,16},{8,20},{12,24},{16,28},{20,32},{24,36},{28,40},{32,4... | collective-permute-start | bytes 1572872 | tf_op jit(solution)/shard_map/ppermute | solution.py:38
  6.1 1.4 %fusion = (s32[1,1]{1,0:T(1,128)}, s32[1,1]{1,0:T(1,128)}, s32[1,1]{1,0:T(1,128)}) fusion(s32[1,3]{1,0:T(1,128)} %param.20), kind=kLoop, calls=%fused_computation.4 | loop fusion | bytes 24 | tf_op jit(solution)/shard_map/slice | solution.py:139
  9.4 2.9 %copy.6 = bf16[1,3,256,2,1024]{4,2,3,1,0:T(8,128)(2,1)S(1)} copy(bf16[1,3,256,2,1024]{4,3,2,1,0:T(2,128)(2,1)} %param.19) | data formatting | bytes 6291456 | tf_op args[1]
  12.3 0.1 pad_add_fusion.places_ref
  12.4 17.9 %collective-permute-done.27 = bf16[1024,256]{1,0:T(8,128)(2,1)} collective-permute-done((bf16[1024,256]{1,0:T(8,128)(2,1)}, bf16[1024,256]{1,0:T(8,128)(2,1)}, u32[]{:S(2)}, u32[]{:S(2)}) %collective-permute-start.27) | collective-permute-done | bytes 524320 | tf_op jit(solution)/shard_map/ppermute | solution.py:38
  30.3 1.9 %collective-permute-start.28 = (bf16[1024,256]{1,0:T(8,128)(2,1)}, bf16[1024,256]{1,0:T(8,128)(2,1)}, u32[]{:S(2)}, u32[]{:S(2)}) collective-permute-start(bf16[1024,256]{1,0:T(8,128)(2,1)} %collective-permute-done.27), channel_id=1, source_target_pairs={{0,16},{4,20},{8,24},{12,28},{16,32},{20,36},{24,40},{28,44},{32,4... | collective-permute-start | bytes 1572872 | tf_op jit(solution)/shard_map/ppermute | solution.py:38
  32.2 36.8 %conditional.1 = (bf16[1024,256]{1,0:T(8,128)(2,1)}, bf16[1024,256]{1,0:T(8,128)(2,1)}, bf16[64,256]{1,0:T(8,128)(2,1)S(1)}, bf16[64,256]{1,0:T(8,128)(2,1)S(1)}) conditional(s32[]{:T(128)} %clamp.3, bf16[1024,256]{1,0:T(8,128)(2,1)} %collective-permute-done.27, (bf16[1024,256]{1,0:T(8,128)(2,1)}, ...), branch_computations={%region_0.1_spmd, %region_1.2_spmd, %region_2.3_spmd, %region_3.4_... | conditional | bytes 6422680 | solution.py:156
  32.2 6.9 %collective-permute-start = (bf16[1024,256]{1,0:T(8,128)(2,1)}, bf16[1024,256]{1,0:T(8,128)(2,1)}, u32[]{:S(2)}, u32[]{:S(2)}) collective-permute-start(bf16[1024,256]{1,0:T(8,128)(2,1)} %param), channel_id=1, source_target_pairs={{0,764},{4,0},{8,4},{12,8},{16,12},{20,16},{24,20},{28,24},{32,28}... | collective-permute-start | bytes 1572872 | tf_op jit(solution)/shard_map/cond/branch_0_fun/ppermute | solution.py:38
  39.1 10.0 %collective-permute-done = bf16[1024,256]{1,0:T(8,128)(2,1)} collective-permute-done((bf16[1024,256]{1,0:T(8,128)(2,1)}, bf16[1024,256]{1,0:T(8,128)(2,1)}, u32[]{:S(2)}, u32[]{:S(2)}) %collective-permute-start) | collective-permute-done | bytes 524320 | tf_op jit(solution)/shard_map/cond/branch_0_fun/ppermute | solution.py:38
  49.1 10.1 %collective-permute-start.1 = (bf16[1024,256]{1,0:T(8,128)(2,1)}, bf16[1024,256]{1,0:T(8,128)(2,1)}, u32[]{:S(2)}, u32[]{:S(2)}) collective-permute-start(bf16[1024,256]{1,0:T(8,128)(2,1)} %collective-permute-done), channel_id=1, source_target_pairs={{0,764},{4,0},{8,4},{12,8},{16,12},{20,16},{24,20},{28,24},{32,28}... | collective-permute-start | bytes 1572872 | tf_op jit(solution)/shard_map/cond/branch_0_fun/ppermute | solution.py:38
  59.2 0.8 slice.109
  60.0 8.3 %collective-permute-done.1 = bf16[1024,256]{1,0:T(8,128)(2,1)} collective-permute-done((bf16[1024,256]{1,0:T(8,128)(2,1)}, bf16[1024,256]{1,0:T(8,128)(2,1)}, u32[]{:S(2)}, u32[]{:S(2)}) %collective-permute-start.1) | collective-permute-done | bytes 524320 | tf_op jit(solution)/shard_map/cond/branch_0_fun/ppermute | solution.py:38
  68.2 0.8 slice.108
  69.0 0.0 collective-permute-done.28.far_ref
  69.0 0.8 slice.133
  69.8 13.3 %all_gather.3.rows_ref = bf16[256,768]{1,0:T(8,128)(2,1)S(1)} all-gather(bf16[64,768]{1,0:T(8,128)(2,1)S(1)} %pad_maximum_fusion), channel_id=1, replica_groups=mesh['ka'=192,'pt'=4] {'pt'}, dimensions={0}, use_global_device_ids=true | all-gather | bytes 491520 | tf_op jit(solution)/shard_map/all_gather | solution.py:56
  83.1 5.1 %shard_map.37 = bf16[256,256]{1,0:T(8,128)(2,1)S(1)} custom-call(s32[3]{0:T(128)S(1)} %pad_add_fusion.places_ref, bf16[1024,256]{1,0:T(8,128)(2,1)} %collective-permute-done.28.far_ref, bf16[1024,256]{1,0:T(8,128)(2,1)} %get-tuple-element.63.low_ref, bf16[1024,256]{1,0:T(8,128)(2,1)} %get-tuple-element.64.high_ref, bf16[256,768]{1,0:T(8,128)(2,1)S(1)} %all_gather.3.rows_ref, ...), custom_call_target="tpu_custom_call" | custom-call | flops 1610612736 | bytes 4718592 | tf_op jit(solution)/shard_map/pallas_call | solution.py:112
  88.2 11.9 %all_to_all.5 = bf16[4,64,256]{2,1,0:T(8,128)(2,1)S(1)} all-to-all(bf16[4,64,256]{2,1,0:T(8,128)(2,1)S(1)} %bitcast.15), channel_id=1, replica_groups=mesh['ka'=192,'pt'=4] {'pt'}, dimensions={0} | all-to-all | bytes 262144 | tf_op jit(solution)/shard_map/all_to_all | solution.py:44
  100.1 0.6 convert_reduce_fusion
  (1 shorter events, 0.0 us)
Async XLA Ops:
  0.0 30.3 %collective-permute-start.27 = (bf16[1024,256]{1,0:T(8,128)(2,1)}, bf16[1024,256]{1,0:T(8,128)(2,1)}, u32[]{:S(2)}, u32[]{:S(2)}) collective-permute-start(bf16[1024,256]{1,0:T(8,128)(2,1)} %bitcast.16), channel_id=1, source_target_pairs={{0,12},{4,16},{8,20},{12,24},{16,28},{20,32},{24,36},{28,40},{32,4... | collective-permute-start | bytes 1572872 | tf_op jit(solution)/shard_map/ppermute | solution.py:38
  30.3 38.7 %collective-permute-start.28 = (bf16[1024,256]{1,0:T(8,128)(2,1)}, bf16[1024,256]{1,0:T(8,128)(2,1)}, u32[]{:S(2)}, u32[]{:S(2)}) collective-permute-start(bf16[1024,256]{1,0:T(8,128)(2,1)} %collective-permute-done.27), channel_id=1, source_target_pairs={{0,16},{4,20},{8,24},{12,28},{16,32},{20,36},{24,40},{28,44},{32,4... | collective-permute-start | bytes 1572872 | tf_op jit(solution)/shard_map/ppermute | solution.py:38
  32.2 16.8 %collective-permute-start = (bf16[1024,256]{1,0:T(8,128)(2,1)}, bf16[1024,256]{1,0:T(8,128)(2,1)}, u32[]{:S(2)}, u32[]{:S(2)}) collective-permute-start(bf16[1024,256]{1,0:T(8,128)(2,1)} %param), channel_id=1, source_target_pairs={{0,764},{4,0},{8,4},{12,8},{16,12},{20,16},{24,20},{28,24},{32,28}... | collective-permute-start | bytes 1572872 | tf_op jit(solution)/shard_map/cond/branch_0_fun/ppermute | solution.py:38
  49.1 19.2 %collective-permute-start.1 = (bf16[1024,256]{1,0:T(8,128)(2,1)}, bf16[1024,256]{1,0:T(8,128)(2,1)}, u32[]{:S(2)}, u32[]{:S(2)}) collective-permute-start(bf16[1024,256]{1,0:T(8,128)(2,1)} %collective-permute-done), channel_id=1, source_target_pairs={{0,764},{4,0},{8,4},{12,8},{16,12},{20,16},{24,20},{28,24},{32,28}... | collective-permute-start | bytes 1572872 | tf_op jit(solution)/shard_map/cond/branch_0_fun/ppermute | solution.py:38

commit v3 on v2

--- a/solution.py
+++ b/solution.py
@@ -23,7 +23,7 @@
     (1, 5): ((1, 0), (5, 1)),
     (2, 5): ((2, 3), (5, 2)),
     (3, 5): ((2, 3), (5, 2)),
-    (4, 5): ((4, 0), (5, 4)),
+    (4, 5): ((2, 3), (4, 0), (5, 2)),
     (1, 6): ((6, 3), (1, 0)),
     (2, 6): ((6, 3), (2, 3)),
     (3, 6): ((6, 3),),
@@ -51,8 +51,30 @@
     return held[low], held[high]
 
 
+def rows_kernel(*refs):
+    *block_refs, rows_ref, sems = refs
+    width = rows_ref.shape[1] // len(block_refs)
+    copies = [
+        pltpu.make_async_copy(
+            block_ref.at[0:MU_DEV, :], rows_ref.at[:, at * width:(at + 1) * width], sems.at[at]
+        )
+        for at, block_ref in enumerate(block_refs)
+    ]
+    for copy in copies:
+        copy.start()
+    for copy in copies:
+        copy.wait()
+
+
 def windows_of(blocks, axis):
-    rows = jnp.concatenate([block[:MU_DEV] for block in blocks], 1)
+    width = blocks[0].shape[1]
+    rows = pl.pallas_call(
+        rows_kernel,
+        out_shape=jax.ShapeDtypeStruct((MU_DEV, len(blocks) * width), blocks[0].dtype),
+        in_specs=[pl.BlockSpec(memory_space=pl.ANY)] * len(blocks),
+        out_specs=pl.BlockSpec(memory_space=pltpu.VMEM),
+        scratch_shapes=[pltpu.SemaphoreType.DMA((len(blocks),))],
+    )(*blocks)
     return lax.all_gather(rows, axis, axis=0, tiled=True)
 
 

time: 101 us -> 105 us (1.040)
  waiting for transfers between devices: 36.1 us -> 53.2 us
  starting transfers between devices: 24.9 us -> 11.8 us
  local copies, waits for them, and re-layouts: 6.57 us -> 4.28 us
  Pallas kernels: 5.1 us -> 6.55 us
    ppermute x4, waiting for transfers between devices: 36.1 us -> 53.2 us  [passed_along(): return lax.ppermute(value, axis, pairs)]
    ppermute x4, starting transfers between devices: 24.9 us -> 11.8 us  [passed_along(): return lax.ppermute(value, axis, pairs)]
    slice x3 -> x0, local copies, waits for them, and re-layouts: 2.29 us -> none  [windows_of(): rows = jnp.concatenate([block[:MU_DEV] for block in blocks], 1)]
    all_to_all x1, blocking collectives: 11.9 us -> 13.6 us  [summed_over(): return jnp.sum(lax.all_to_all(blocks, axis, 0, 0).astype(jnp.float32), 0)]
    pallas_call x0 -> x1, Pallas kernels: none -> 1.45 us  [windows_of(): pl.pallas_call(rows_kernel, out_shape=jax.ShapeDtypeStruct((MU_DEV, len(b...]
  transfers between devices with their start and end apart: 4 -> 4, of which waited for: 3 -> 3; matrix products, arithmetic and copies ran while one was open for 6% -> 4% of each run, Pallas kernels for 0% -> 0%
where the time goes in v3:
time: 105 us
  waiting for transfers between devices  53.2 us (51%)
  blocking collectives  26.1 us (25%)
  starting transfers between devices  11.8 us (11%)
  Pallas kernels  6.55 us (6%)
  local copies, waits for them, and re-layouts  4.28 us (4%)
  between operations  2.12 us (2%)
    ppermute x4, waiting for transfers between devices, passed_along(): return lax.ppermute(value, axis, pairs)  53.2 us
    all_to_all x1, blocking collectives, summed_over(): return jnp.sum(lax.all_to_all(blocks, axis, 0, 0).astype(jnp.float32), 0)  13.6 us
    all_gather x1, blocking collectives, windows_of(): return lax.all_gather(rows, axis, axis=0, tiled=True)  12.5 us
    ppermute x4, starting transfers between devices, passed_along(): return lax.ppermute(value, axis, pairs)  11.8 us
    pallas_call x1, Pallas kernels, exchanged_here(): pl.pallas_call(exchange_kernel, out_shape=jax.ShapeDtypeStruct((row_total...  5.1 us
    unnamed x1, local copies, waits for them, and re-layouts  2.86 us
  transfers between devices with their start and end apart: 4, of which 3 were waited for; matrix products, arithmetic and copies ran while one was open for 4% of the time, Pallas kernels for 0%

profile of v3, /device:TPU:1, one launch (start us, length us, event | category | flops | bytes accessed | tf_op | source)
XLA Modules:
  0.0 104.8 jit_solution(7199203442972018376)
XLA Ops:
  0.0 6.1 %collective-permute-start.28 = (bf16[1024,256]{1,0:T(8,128)(2,1)}, bf16[1024,256]{1,0:T(8,128)(2,1)}, u32[]{:S(2)}, u32[]{:S(2)}) collective-permute-start(bf16[1024,256]{1,0:T(8,128)(2,1)} %bitcast.16), channel_id=1, source_target_pairs={{0,12},{4,16},{8,20},{12,24},{16,28},{20,32},{24,36},{28,40},{32,4... | collective-permute-start | bytes 1572872 | tf_op jit(solution)/shard_map/ppermute | solution.py:38
  6.1 1.4 %fusion = (s32[1,1]{1,0:T(1,128)}, s32[1,1]{1,0:T(1,128)}, s32[1,1]{1,0:T(1,128)}) fusion(s32[1,3]{1,0:T(1,128)} %param.20), kind=kLoop, calls=%fused_computation.3 | loop fusion | bytes 24 | tf_op jit(solution)/shard_map/slice | solution.py:161
  9.5 2.9 %copy.6 = bf16[1,3,256,2,1024]{4,2,3,1,0:T(8,128)(2,1)S(1)} copy(bf16[1,3,256,2,1024]{4,3,2,1,0:T(2,128)(2,1)} %param.19) | data formatting | bytes 6291456 | tf_op args[1]
  12.4 0.1 pad_add_fusion.places_ref
  12.5 17.8 %collective-permute-done.28 = bf16[1024,256]{1,0:T(8,128)(2,1)} collective-permute-done((bf16[1024,256]{1,0:T(8,128)(2,1)}, bf16[1024,256]{1,0:T(8,128)(2,1)}, u32[]{:S(2)}, u32[]{:S(2)}) %collective-permute-start.28) | collective-permute-done | bytes 524320 | tf_op jit(solution)/shard_map/ppermute | solution.py:38
  30.3 1.9 %collective-permute-start.29 = (bf16[1024,256]{1,0:T(8,128)(2,1)}, bf16[1024,256]{1,0:T(8,128)(2,1)}, u32[]{:S(2)}, u32[]{:S(2)}) collective-permute-start(bf16[1024,256]{1,0:T(8,128)(2,1)} %collective-permute-done.28), channel_id=1, source_target_pairs={{0,16},{4,20},{8,24},{12,28},{16,32},{20,36},{24,40},{28,44},{32,4... | collective-permute-start | bytes 1572872 | tf_op jit(solution)/shard_map/ppermute | solution.py:38
  32.2 39.3 %conditional.1 = (bf16[1024,256]{1,0:T(8,128)(2,1)}, bf16[1024,256]{1,0:T(8,128)(2,1)}) conditional(s32[]{:T(128)} %clamp.3, bf16[1024,256]{1,0:T(8,128)(2,1)} %collective-permute-done.28, (bf16[1024,256]{1,0:T(8,128)(2,1)}, bf16[1024,256]{1,0:T(8,128)(2,1)}) %tuple.86, ...), branch_computations={%region_0.1_spmd, %region_1.2_spmd, %region_2.3_spmd, %region_3.4_... | conditional | bytes 6291592 | solution.py:178
  32.3 1.9 %collective-permute-start.24 = (bf16[1024,256]{1,0:T(8,128)(2,1)}, bf16[1024,256]{1,0:T(8,128)(2,1)}, u32[]{:S(2)}, u32[]{:S(2)}) collective-permute-start(bf16[1024,256]{1,0:T(8,128)(2,1)} %get-tuple-element.53), channel_id=1, source_target_pairs={{0,16},{4,20},{8,24},{12,28},{16,32},{20,36},{24,40},{28,44},{32,4... | collective-permute-start | bytes 1572872 | tf_op jit(solution)/shard_map/cond/branch_13_fun/ppermute | solution.py:38
  34.2 1.9 %collective-permute-start.25 = (bf16[1024,256]{1,0:T(8,128)(2,1)}, bf16[1024,256]{1,0:T(8,128)(2,1)}, u32[]{:S(2)}, u32[]{:S(2)}) collective-permute-start(bf16[1024,256]{1,0:T(8,128)(2,1)} %get-tuple-element.54), channel_id=1, source_target_pairs={{0,12},{4,16},{8,20},{12,24},{16,28},{20,32},{24,36},{28,40},{32,4... | collective-permute-start | bytes 1572872 | tf_op jit(solution)/shard_map/cond/branch_13_fun/ppermute | solution.py:38
  36.1 23.1 %collective-permute-done.24 = bf16[1024,256]{1,0:T(8,128)(2,1)} collective-permute-done((bf16[1024,256]{1,0:T(8,128)(2,1)}, bf16[1024,256]{1,0:T(8,128)(2,1)}, u32[]{:S(2)}, u32[]{:S(2)}) %collective-permute-start.24) | collective-permute-done | bytes 524320 | tf_op jit(solution)/shard_map/cond/branch_13_fun/ppermute | solution.py:38
  59.2 12.3 %collective-permute-done.25 = bf16[1024,256]{1,0:T(8,128)(2,1)} collective-permute-done((bf16[1024,256]{1,0:T(8,128)(2,1)}, bf16[1024,256]{1,0:T(8,128)(2,1)}, u32[]{:S(2)}, u32[]{:S(2)}) %collective-permute-start.25) | collective-permute-done | bytes 524320 | tf_op jit(solution)/shard_map/cond/branch_13_fun/ppermute | solution.py:38
  71.5 0.0 collective-permute-done.29.refs_0_.far_ref
  71.5 1.5 %shard_map.37 = bf16[64,768]{1,0:T(8,128)(2,1)} custom-call(bf16[1024,256]{1,0:T(8,128)(2,1)} %collective-permute-done.29.refs_0_.far_ref, bf16[1024,256]{1,0:T(8,128)(2,1)} %get-tuple-element.64.refs_1_.low_ref, bf16[1024,256]{1,0:T(8,128)(2,1)} %get-tuple-element.65.refs_2_.high_ref), custom_call_target="tpu_custom_call" | custom-call | tf_op jit(solution)/shard_map/pallas_call | solution.py:71
  73.0 12.5 %all_gather.3.rows_ref = bf16[256,768]{1,0:T(8,128)(2,1)S(1)} all-gather(bf16[64,768]{1,0:T(8,128)(2,1)} %shard_map.37), channel_id=1, replica_groups=mesh['ka'=192,'pt'=4] {'pt'}, dimensions={0}, use_global_device_ids=true | all-gather | bytes 491520 | tf_op jit(solution)/shard_map/all_gather | solution.py:78
  85.5 5.1 %shard_map.38 = bf16[256,256]{1,0:T(8,128)(2,1)S(1)} custom-call(s32[3]{0:T(128)S(1)} %pad_add_fusion.places_ref, bf16[1024,256]{1,0:T(8,128)(2,1)} %collective-permute-done.29.refs_0_.far_ref, bf16[1024,256]{1,0:T(8,128)(2,1)} %get-tuple-element.64.refs_1_.low_ref, bf16[1024,256]{1,0:T(8,128)(2,1)} %get-tuple-element.65.refs_2_.high_ref, ...), custom_call_target="tpu_custom_call" | custom-call | flops 1610612736 | bytes 4718592 | tf_op jit(solution)/shard_map/pallas_call | solution.py:134
  90.6 13.6 %all_to_all.5 = bf16[4,64,256]{2,1,0:T(8,128)(2,1)S(1)} all-to-all(bf16[4,64,256]{2,1,0:T(8,128)(2,1)S(1)} %bitcast.15), channel_id=1, replica_groups=mesh['ka'=192,'pt'=4] {'pt'}, dimensions={0} | all-to-all | bytes 262144 | tf_op jit(solution)/shard_map/all_to_all | solution.py:44
  104.2 0.6 convert_reduce_fusion
Async XLA Ops:
  0.0 30.3 %collective-permute-start.28 = (bf16[1024,256]{1,0:T(8,128)(2,1)}, bf16[1024,256]{1,0:T(8,128)(2,1)}, u32[]{:S(2)}, u32[]{:S(2)}) collective-permute-start(bf16[1024,256]{1,0:T(8,128)(2,1)} %bitcast.16), channel_id=1, source_target_pairs={{0,12},{4,16},{8,20},{12,24},{16,28},{20,32},{24,36},{28,40},{32,4... | collective-permute-start | bytes 1572872 | tf_op jit(solution)/shard_map/ppermute | solution.py:38
  30.3 41.2 %collective-permute-start.29 = (bf16[1024,256]{1,0:T(8,128)(2,1)}, bf16[1024,256]{1,0:T(8,128)(2,1)}, u32[]{:S(2)}, u32[]{:S(2)}) collective-permute-start(bf16[1024,256]{1,0:T(8,128)(2,1)} %collective-permute-done.28), channel_id=1, source_target_pairs={{0,16},{4,20},{8,24},{12,28},{16,32},{20,36},{24,40},{28,44},{32,4... | collective-permute-start | bytes 1572872 | tf_op jit(solution)/shard_map/ppermute | solution.py:38
  32.3 27.0 %collective-permute-start.24 = (bf16[1024,256]{1,0:T(8,128)(2,1)}, bf16[1024,256]{1,0:T(8,128)(2,1)}, u32[]{:S(2)}, u32[]{:S(2)}) collective-permute-start(bf16[1024,256]{1,0:T(8,128)(2,1)} %get-tuple-element.53), channel_id=1, source_target_pairs={{0,16},{4,20},{8,24},{12,28},{16,32},{20,36},{24,40},{28,44},{32,4... | collective-permute-start | bytes 1572872 | tf_op jit(solution)/shard_map/cond/branch_13_fun/ppermute | solution.py:38
  34.2 37.3 %collective-permute-start.25 = (bf16[1024,256]{1,0:T(8,128)(2,1)}, bf16[1024,256]{1,0:T(8,128)(2,1)}, u32[]{:S(2)}, u32[]{:S(2)}) collective-permute-start(bf16[1024,256]{1,0:T(8,128)(2,1)} %get-tuple-element.54), channel_id=1, source_target_pairs={{0,12},{4,16},{8,20},{12,24},{16,28},{20,32},{24,36},{28,40},{32,4... | collective-permute-start | bytes 1572872 | tf_op jit(solution)/shard_map/cond/branch_13_fun/ppermute | solution.py:38
